TPU v7x, 32 devices: a whole 2x2x4 slice. The times are simulated.
32 devices in a mesh: men: 8 (over y, x, core), women: 4 (over z).
Axes of the slice: x: 2, y: 2, z: 4, core: 2. Of those that a mesh axis runs over, the one named last changes fastest.
Arguments:
- men_embed: bfloat16 [16384, 128], P(('men', 'women')), may hold values from -4 to 4
- women_embed: bfloat16 [4096, 128], P(('women', 'men')), may hold values from -4 to 4
- men_count: int32 [16384], P('men'), may hold values from 1 to 297, as said below
- women_count: int32 [4096], P('women'), may hold values from 1 to 299
- women_root: float32 [4096], P('women'), may hold values from 0.5 to 6, as said below
- men_cotangent: float32 [16384], P('men'), may hold values from -300 to 300
- women_cotangent: float32 [4096], P('women'), may hold values from 24 to 864, as said below
Outputs:
- men_grad: float32 [16384, 128], P(('men', 'women'))
- women_grad: float32 [4096, 128], P(('women', 'men'))
Inputs may be any that keep to these rules, and one draw needn't show every extreme that they name: `men_count`: integer masses of the male types. `women_root`: positive. `women_cotangent`: positive.
All inputs are finite; a program needn't handle non-finite values.
Results may differ from a plain program's by a relative error of at most 0.0031.
Values may be sent and summed in bfloat16 or wider, within the bound.
A program may use at most 64 MiB of HBM per device.

v0:
```python
import jax
import jax.numpy as jnp
from jax import lax
from jax.sharding import PartitionSpec as P


def kernel_tile(men_rows, women_block):
    surplus = lax.dot_general(
        men_rows, women_block, (((1,), (1,)), ((), ())), preferred_element_type=jnp.float32
    )
    return jnp.exp(0.5 * surplus)


def body(
    men_embed, women_embed, men_count, women_count, women_root, men_cotangent, women_cotangent
):
    men_rows = lax.all_gather(men_embed, "women", axis=0, tiled=True)
    women_rows = lax.all_gather(women_embed, "men", axis=0, tiled=True)
    men_mass = men_count.astype(jnp.float32)
    women_mass = women_count.astype(jnp.float32)
    stored = kernel_tile(men_rows, women_rows)

    def sweep(work):
        return work(stored, women_rows, 0)

    def first_work(kernel, women_block, col_start):
        weighted = kernel * women_root[None, :]
        product = jnp.dot(
            weighted.astype(jnp.bfloat16), women_block, preferred_element_type=jnp.float32
        )
        return ((jnp.sum(weighted, axis=1), product), ())

    row_partial, weighted_v = sweep(first_work)[0]
    row_mass = lax.psum(row_partial, "women")
    men_disc = jnp.sqrt(row_mass * row_mass + 4.0 * men_mass)
    men_root = 2.0 * men_mass / (row_mass + men_disc)

    def second_work(kernel, women_block, col_start):
        return ((), (jnp.sum(kernel * men_root[:, None], axis=0),))

    col_partial = sweep(second_work)[1][0]
    col_mass = lax.psum(col_partial, "men")
    women_disc = jnp.sqrt(col_mass * col_mass + 4.0 * women_mass)
    col_grad = -women_cotangent / women_disc

    def third_work(kernel, women_block, col_start):
        weighted = kernel * col_grad[None, :]
        product = jnp.dot(
            weighted.astype(jnp.bfloat16), women_block, preferred_element_type=jnp.float32
        )
        return ((jnp.sum(weighted, axis=1), product), ())

    row_back, direct_v = sweep(third_work)[0]
    row_cot = lax.psum(row_back, "women")
    row_grad = -(men_cotangent + men_root * row_cot) / men_disc
    men_term = 0.5 * (row_grad[:, None] * weighted_v + men_root[:, None] * direct_v)
    men_grad = lax.psum_scatter(men_term, "women", scatter_dimension=0, tiled=True)

    def fourth_work(kernel, women_block, col_start):
        tangent = (
            0.5
            * kernel
            * (row_grad[:, None] * women_root[None, :] + men_root[:, None] * col_grad[None, :])
        ).astype(jnp.bfloat16)
        return (
            (),
            (
                lax.dot_general(
                    tangent, men_rows, (((0,), (0,)), ((), ())), preferred_element_type=jnp.float32
                ),
            ),
        )

    women_terms = sweep(fourth_work)[1][0]
    women_grad = lax.psum_scatter(women_terms, "men", scatter_dimension=0, tiled=True)
    return (men_grad, women_grad)


def solution(mesh):
    return jax.shard_map(
        body,
        mesh=mesh,
        in_specs=(
            P(("men", "women"), None),
            P(("women", "men"), None),
            P("men"),
            P("women"),
            P("women"),
            P("men"),
            P("women"),
        ),
        out_specs=(P(("men", "women"), None), P(("women", "men"), None)),
        check_vma=False,
    )
```

profile of v0, /device:TPU:0, one launch (start us, length us, event | category | flops | bytes accessed | tf_op | source)
XLA Modules:
  0.0 156.1 jit_solution(900042183173086591)
XLA Ops:
  7.2 0.0 copy-start.1
  7.2 0.0 reduce-scatter.5.cloned.1.call-start
  7.2 11.0 %all_gather.7 = bf16[1024,128]{1,0:T(8,128)(2,1)S(1)} all-gather(bf16[128,128]{1,0:T(8,128)(2,1)} %param.8), channel_id=1, replica_groups=mesh['men'=8,'women'=4] {'men'}, dimensions={0}, use_global_device_ids=true | all-gather | bytes 294912 | tf_op jit(solution)/shard_map/all_gather | solution.py:18
  18.2 16.6 %all_gather.6 = bf16[2048,128]{1,0:T(8,128)(2,1)S(1)} all-gather(bf16[512,128]{1,0:T(8,128)(2,1)} %param.7), channel_id=1, replica_groups=mesh['men'=8,'women'=4] {'women'}, dimensions={0}, use_global_device_ids=true | all-gather | bytes 655360 | tf_op jit(solution)/shard_map/all_gather | solution.py:17
  34.7 0.0 copy-start.3
  34.7 0.0 copy-start.4
  34.8 4.8 %multiply_reduce_fusion.2 = (f32[2048]{0:T(1024)S(1)}, f32[2048,1024]{0,1:T(8,128)}) fusion(f32[1024]{0:T(1024)} %param.11, bf16[2048,128]{1,0:T(8,128)(2,1)S(1)} %all_gather.6, bf16[1024,128]{1,0:T(8,128)(2,1)S(1)} %all_gather.7), kind=kOutput, calls=%fused_computation.6 | convolution fusion | flops 543160320 | bytes 9187328 | tf_op jit(solution)/shard_map/dot_general | solution.py:8
  39.6 12.2 %psum.21 = f32[2048]{0:T(1024)S(1)} all-reduce(f32[2048]{0:T(1024)S(1)} %get-tuple-element.2), channel_id=1, replica_groups=mesh['men'=8,'women'=4] {'women'}, use_global_device_ids=true, to_apply=%region_1.0 | all-reduce | flops 2048 | bytes 16384 | tf_op jit(solution)/shard_map/psum | solution.py:34
  51.8 0.0 copy-done.1
  51.8 0.0 copy-start.2
  51.8 0.0 copy-start
  51.9 4.0 %multiply_reduce_fusion = f32[1024]{0:T(1024)S(1)} fusion(f32[2048,1024]{0,1:T(8,128)} %get-tuple-element.3, f32[2048]{0:T(1024)S(1)} %add_divide_fusion), kind=kLoop, calls=%fused_computation.1 | loop fusion | flops 4193280 | bytes 8400896 | tf_op jit(solution)/shard_map/reduce_sum | solution.py:39
  55.9 11.8 %psum.22 = f32[1024]{0:T(1024)S(1)} all-reduce(f32[1024]{0:T(1024)S(1)} %multiply_reduce_fusion), channel_id=1, replica_groups=mesh['men'=8,'women'=4] {'men'}, use_global_device_ids=true, to_apply=%region_3.0 | all-reduce | flops 1024 | bytes 8192 | tf_op jit(solution)/shard_map/psum | solution.py:42
  67.7 0.0 copy-done.3
  67.7 0.0 copy-done.4
  67.7 4.0 %multiply_reduce_fusion.1 = f32[2048]{0:T(1024)S(1)} fusion(f32[2048,1024]{0,1:T(8,128)} %get-tuple-element.3, f32[1024]{0:T(1024)S(1)} %rsqrt_multiply_fusion), kind=kLoop, calls=%fused_computation.4 | loop fusion | flops 4192256 | bytes 8400896 | tf_op jit(solution)/shard_map/reduce_sum | solution.py:51
  71.7 8.5 %psum.23 = f32[2048]{0:T(1024)S(1)} all-reduce(f32[2048]{0:T(1024)S(1)} %multiply_reduce_fusion.1), channel_id=1, replica_groups=mesh['men'=8,'women'=4] {'women'}, use_global_device_ids=true, to_apply=%region_5.0 | all-reduce | flops 2048 | bytes 16384 | tf_op jit(solution)/shard_map/psum | solution.py:54
  80.2 0.0 copy-done.2
  80.3 0.0 copy-done
  80.3 5.9 %fusion.4 = f32[1024,128]{1,0:T(8,128)} fusion(bf16[2048,128]{1,0:T(8,128)(2,1)S(1)} %all_gather.6, f32[2048,1024]{0,1:T(8,128)} %get-tuple-element.3, f32[2048]{0:T(1024)S(1)} %negate_divide_fusion, f32[1024]{0:T(1024)S(1)} %rsqrt_multiply_fusion, f32[2048]{0:T(1024)S(1)} %add_divide_fusion, f32[1024]{0:T(1024)S(1)} %copy-done), kind=kOutput, calls=%fused_computation.11 | convolution fusion | flops 549453824 | bytes 9461760 | tf_op jit(solution)/shard_map/dot_general | solution.py:68
  86.2 0.0 reduce-scatter.5.cloned.1.call-update
  86.2 0.0 reduce-scatter.3.cloned.1.call-start
  86.3 5.0 %fusion.5 = f32[2048,128]{1,0:T(8,128)S(1)} fusion(bf16[1024,128]{1,0:T(8,128)(2,1)S(1)} %all_gather.7, f32[2048,1024]{0,1:T(8,128)} %get-tuple-element.3, f32[1024]{0:T(1024)S(1)} %rsqrt_multiply_fusion, f32[2048]{0:T(1024)S(1)} %add_divide_fusion), kind=kOutput, calls=%fused_computation.12 | convolution fusion | flops 541327360 | bytes 9711616 | tf_op jit(solution)/shard_map/dot_general | solution.py:48
  91.2 6.2 %fusion.8 = f32[2048,128]{1,0:T(8,128)} fusion(f32[2048,128]{1,0:T(8,128)S(1)} %fusion.5, bf16[1024,128]{1,0:T(8,128)(2,1)S(1)} %all_gather.7, f32[2048,1024]{0,1:T(8,128)} %get-tuple-element.3, f32[1024]{0:T(1024)S(1)} %copy-done, f32[2048]{0:T(1024)S(1)} %negate_divide_fusion), kind=kOutput, calls=%fused_computation.15 | convolution fusion | flops 541851648 | bytes 10760192 | tf_op jit(solution)/shard_map/dot_general | solution.py:28
  97.4 0.0 reduce-scatter.3.cloned.1.call-update
  97.5 21.6 %reduce-scatter.5.cloned.1.call-done = f32[128,128]{1,0:T(8,128)} async-done(((f32[1024,128]{1,0:T(8,128)}), f32[128,128]{1,0:T(8,128)}) %reduce-scatter.5.cloned.1.call-update) | async-done | bytes 65552 | tf_op jit(solution)/shard_map/reduce_scatter | solution.py:75
  119.1 30.1 %reduce-scatter.3.cloned.1.call-done = f32[512,128]{1,0:T(8,128)} async-done(((f32[2048,128]{1,0:T(8,128)}), f32[512,128]{1,0:T(8,128)}) %reduce-scatter.3.cloned.1.call-update) | async-done | bytes 262160 | tf_op jit(solution)/shard_map/reduce_scatter | solution.py:57
  (3 shorter events, 0.0 us)
Async XLA Ops:
  7.2 44.6 %copy-start.1 = (s32[2048]{0:T(1024)S(1)}, s32[2048]{0:T(1024)}, u32[]{:S(2)}) copy-start(s32[2048]{0:T(1024)} %param.9) | copy-start | bytes 24580
  7.2 111.9 %reduce-scatter.5.cloned.1.call-start = ((), (), s32[]{:S(2)}) async-start(), calls=%async_computation.3 | async-start | bytes 589824 | tf_op jit(solution)/shard_map/reduce_scatter | solution.py:75
  34.7 32.9 %copy-start.3 = (s32[1024]{0:T(1024)S(1)}, s32[1024]{0:T(1024)}, u32[]{:S(2)}) copy-start(s32[1024]{0:T(1024)} %param.10) | copy-start | bytes 12292
  34.7 32.9 %copy-start.4 = (f32[1024]{0:T(1024)S(1)}, f32[1024]{0:T(1024)}, u32[]{:S(2)}) copy-start(f32[1024]{0:T(1024)} %param.13) | copy-start | bytes 12292
  51.8 28.4 %copy-start.2 = (f32[2048]{0:T(1024)S(1)}, f32[2048]{0:T(1024)}, u32[]{:S(2)}) copy-start(f32[2048]{0:T(1024)} %param.12) | copy-start | bytes 24580
  51.8 28.4 %copy-start = (f32[1024]{0:T(1024)S(1)}, f32[1024]{0:T(1024)}, u32[]{:S(2)}) copy-start(f32[1024]{0:T(1024)} %param.11) | copy-start | bytes 12292
  86.2 63.0 %reduce-scatter.3.cloned.1.call-start = ((), (), s32[]{:S(2)}) async-start(), calls=%async_computation.2 | async-start | bytes 1310720 | tf_op jit(solution)/shard_map/reduce_scatter | solution.py:57
Sparse Core Ops, SparseCore 0:
  86.3 32.7 reduce-scatter.4
  122.0 27.1 reduce-scatter.2
where the time goes:
time: 157 us; the launch traced here: 156 us
  blocking collectives  60.1 us (38%)
  waiting for transfers between devices  51.8 us (33%)
  matrix products  21.9 us (14%)
  between operations  14.1 us (9%)
  other arithmetic  8.05 us (5%)
    reduce_scatter x1, waiting for transfers between devices, body(): lax.psum_scatter(men_term, 'women', scatter_dimension=0, tiled=True)  30.1 us
    reduce_scatter x1, waiting for transfers between devices, body(): lax.psum_scatter(women_terms, 'men', scatter_dimension=0, tiled=True)  21.6 us
    all_gather x1, blocking collectives, body(): men_rows = lax.all_gather(men_embed, 'women', axis=0, tiled=True)  16.6 us
    psum x1, blocking collectives, body(): row_mass = lax.psum(row_partial, 'women')  12.2 us
    psum x1, blocking collectives, body(): col_mass = lax.psum(col_partial, 'men')  11.8 us
    all_gather x1, blocking collectives, body(): women_rows = lax.all_gather(women_embed, 'men', axis=0, tiled=True)  11 us
    psum x1, blocking collectives, body(): row_cot = lax.psum(row_back, 'women')  8.52 us
    dot_general x1, matrix products, first_work(): jnp.dot(weighted.astype(jnp.bfloat16), women_block, preferred_element_typ...  6.19 us
  transfers between devices with their start and end apart: 2, of which 2 were waited for; matrix products, arithmetic and copies ran while one was open for 7% of the time, Pallas kernels for 0%

commit v1 on v0

v1 whole, which is shorter than its diff:
```python
import functools
import math

import jax
import jax.numpy as jnp
from jax import lax
from jax.experimental import pallas as pl
from jax.experimental.pallas import tpu as pltpu
from jax.sharding import PartitionSpec as P

F32 = jnp.float32
BF16 = jnp.bfloat16
MESH = pl.DeviceIdType.MESH
HALF_LOG2E = 0.5 * math.log2(math.e)


def loop(start, stop, step_fn):
    if stop - start <= 8:
        for i in range(start, stop):
            step_fn(i)
    else:
        lax.fori_loop(start, stop, lambda i, _: (step_fn(i), 0)[1], 0)


def kernel(
    n_men, n_women,
    men_ref, women_ref, count_ref, cot_ref, root_ref, wcount_ref, wcot_ref,
    men_out, women_out,
    wbuf, kmat, rootbuf, gradbuf, rootg, gradg, colp, pieces, zsum, psum_, quarter,
    wv, dv, rsum, tang, csend, crecv, keep, xsend, xrecv, zsend, zrecv,
    ag_recv, ag_zsend, ag_xsend, ag_csend,
    root_send, root_recv, cz_send, cz_recv, cp_send, cp_recv, cg_send, cg_recv,
    gc_send, gc_recv, gx_send, gx_recv, gz_send, gz_recv,
):
    rows = men_ref.shape[0]
    width = women_ref.shape[0]
    group = n_women * width
    n_chips = n_men // 2
    chunk = min(rows, 128)
    m = lax.axis_index("men")
    w = lax.axis_index("women")
    c = m // 2
    core = m % 2
    sib = c * 2 + (1 - core)

    def z_to(j):
        return lax.rem(w + j, n_women)

    def z_from(j):
        return lax.rem(w + n_women - j, n_women)

    def chip_to(k):
        return lax.rem(c + k, n_chips)

    def chip_from(k):
        return lax.rem(c + n_chips - k, n_chips)

    def copy(src, dst, send, recv, to_m, to_w):
        return pltpu.make_async_remote_copy(
            src_ref=src, dst_ref=dst, send_sem=send, recv_sem=recv,
            device_id=(to_m, to_w), device_id_type=MESH,
        )

    barrier = pltpu.get_barrier_semaphore()
    loop(1, n_women, lambda j: pl.semaphore_signal(
        barrier, inc=1, device_id=(m, z_to(j)), device_id_type=MESH))
    loop(1, n_men, lambda j: pl.semaphore_signal(
        barrier, inc=1, device_id=(lax.rem(m + j, n_men), w), device_id_type=MESH))
    wbuf[m, w] = women_ref[...]
    rootbuf[w] = root_ref[...]
    pl.semaphore_wait(barrier, n_women + n_men - 2)

    def block_copy(at_m, at_w, send, to_m, to_w):
        return copy(wbuf.at[at_m, at_w], wbuf.at[at_m, at_w], send,
                    ag_recv.at[at_m, at_w], to_m, to_w)

    def z_copy(j):
        return block_copy(m, w, ag_zsend.at[j], m, z_to(j))

    def x_copy(k, j):
        return block_copy(m, z_from(j), ag_xsend.at[k, j], chip_to(k) * 2 + core, w)

    def c_copy(k, j):
        return block_copy(chip_from(k) * 2 + core, z_from(j), ag_csend.at[k, j], sib, w)

    def landed(at_m, at_w):
        block_copy(at_m, at_w, ag_zsend.at[0], sib, w).wait_recv()

    def root_copy(j):
        return copy(rootbuf.at[w], rootbuf.at[w], root_send.at[j], root_recv.at[j], m, z_to(j))

    loop(1, n_women, lambda j: z_copy(j).start())
    loop(1, n_chips, lambda k: x_copy(k, 0).start())
    loop(1, n_women, lambda j: root_copy(j).start())
    c_copy(0, 0).start()

    def column(row):
        return jnp.broadcast_to(row, (128, rows)).T

    mass = column(count_ref[w].astype(F32))
    men_cot = column(cot_ref[w])
    men_t = men_ref[...].astype(F32).T.astype(BF16)
    rsum[...] = jnp.zeros_like(rsum)
    wv[...] = jnp.zeros_like(wv)

    def pass_on(j):
        landed(m, z_from(j))
        loop(1, n_chips, lambda k: x_copy(k, j).start())
        c_copy(0, j).start()

    loop(1, n_women, pass_on)
    loop(1, n_women, lambda j: root_copy(j).wait_recv())

    def spread(buf, out):
        for i in range(n_women):
            out[:, i * width:(i + 1) * width] = buf[i]

    spread(rootbuf, rootg)

    def lanes(values):
        total = values[:, :128]
        for i in range(1, group // 128):
            total = total + values[:, i * 128:(i + 1) * 128]
        return total

    def first(g):
        block = wbuf[g].reshape(group, 128)
        roots = rootg[pl.ds(g, 1), :]
        for r in range(0, rows, chunk):
            at = pl.ds(r, chunk)
            phi = lax.dot_general(men_ref[at, :], block, (((1,), (1,)), ((), ())),
                                  preferred_element_type=F32)
            k = jnp.exp2(phi * HALF_LOG2E)
            kmat[g, at, :] = k
            weighted = k * roots
            rsum[at, :] += lanes(weighted)
            wv[at, :] += jnp.dot(weighted.astype(BF16), block, preferred_element_type=F32)

    def all_landed(at_m):
        loop(0, n_women, lambda i: landed(at_m, i))

    def from_chip(k):
        at_m = chip_from(k) * 2 + core

        def forward(j):
            landed(at_m, z_from(j))
            c_copy(k, j).start()

        loop(0, n_women, forward)
        first(at_m)

    def from_sibling(k):
        at_m = chip_from(k) * 2 + (1 - core)
        all_landed(at_m)
        first(at_m)

    first(m)
    from_sibling(0)
    loop(1, n_chips, from_chip)
    loop(1, n_chips, from_sibling)

    row_mass = jnp.broadcast_to(jnp.sum(rsum[...], axis=1, keepdims=True), (rows, 128))
    men_disc = jnp.sqrt(row_mass * row_mass + 4.0 * mass)
    men_root = 2.0 * mass / (row_mass + men_disc)

    def wide(values):
        return jnp.concatenate([values] * (group // 128), axis=1)

    def second(g):
        total = jnp.zeros((8, group), F32)
        for r in range(0, rows, chunk):
            term = kmat[g, pl.ds(r, chunk), :] * wide(men_root[r:r + chunk])
            total = total + jnp.sum(term.reshape(chunk // 8, 8, group), axis=0)
        colp[pl.ds(g, 1), :] = jnp.sum(total, axis=0, keepdims=True)

    loop(0, n_men, second)

    for i in range(n_women):
        pieces[i] = colp[:, i * width:(i + 1) * width]

    def cz_copy(j):
        return copy(pieces.at[z_to(j)], zsum.at[j], cz_send.at[j], cz_recv.at[j], m, z_to(j))

    loop(1, n_women, lambda j: cz_copy(j).start())
    quarter[...] = pieces[w]

    def add_z(j):
        cz_copy(j).wait_recv()
        quarter[...] += zsum[j]

    loop(1, n_women, add_z)

    def cp_copy(j):
        return copy(quarter, psum_.at[j], cp_send.at[j], cp_recv.at[j],
                    lax.rem(m + j, n_men), w)

    loop(1, n_men, lambda j: cp_copy(j).start())
    psum_[0] = quarter[...]

    def add_p(j):
        cp_copy(j).wait_recv()
        psum_[0] += psum_[j]

    loop(1, n_men, add_p)
    col_mass = psum_[0]
    women_disc = jnp.sqrt(col_mass * col_mass + 4.0 * wcount_ref[...].astype(F32))
    gradbuf[w] = -wcot_ref[...] / women_disc

    def cg_copy(j):
        return copy(gradbuf.at[w], gradbuf.at[w], cg_send.at[j], cg_recv.at[j], m, z_to(j))

    loop(1, n_women, lambda j: cg_copy(j).start())
    rsum[...] = jnp.zeros_like(rsum)
    dv[...] = jnp.zeros_like(dv)
    loop(1, n_women, lambda j: cg_copy(j).wait_recv())
    spread(gradbuf, gradg)

    def third(g):
        block = wbuf[g].reshape(group, 128)
        grads = gradg[pl.ds(g, 1), :]
        for r in range(0, rows, chunk):
            at = pl.ds(r, chunk)
            weighted = kmat[g, at, :] * grads
            rsum[at, :] += lanes(weighted)
            dv[at, :] += jnp.dot(weighted.astype(BF16), block, preferred_element_type=F32)

    loop(0, n_men, third)
    row_cot = jnp.broadcast_to(jnp.sum(rsum[...], axis=1, keepdims=True), (rows, 128))
    row_grad = -(men_cot + men_root * row_cot) / men_disc
    half_grad = 0.5 * row_grad
    half_root = 0.5 * men_root
    men_out[...] = half_grad * wv[...] + half_root * dv[...]

    def fourth(g):
        roots = rootg[pl.ds(g, 1), :]
        grads = gradg[pl.ds(g, 1), :]
        for r in range(0, rows, chunk):
            at = pl.ds(r, chunk)
            scale = wide(half_grad[r:r + chunk]) * roots + wide(half_root[r:r + chunk]) * grads
            tang[at, :] = (kmat[g, at, :] * scale).astype(BF16)
        return jnp.dot(men_t, tang[...], preferred_element_type=F32).T

    def gc_copy(k):
        return copy(csend.at[k], crecv.at[k], gc_send.at[k], gc_recv.at[k], sib, w)

    def gx_copy(k):
        return copy(xsend.at[k], xrecv.at[k], gx_send.at[k], gx_recv.at[k],
                    chip_to(k) * 2 + core, w)

    def gz_copy(j):
        return copy(zsend.at[z_to(j)], zrecv.at[j], gz_send.at[j], gz_recv.at[j], m, z_to(j))

    def chip_terms(k):
        csend[k] = fourth(chip_to(k) * 2 + (1 - core))
        gc_copy(k).start()
        keep[...] = fourth(chip_to(k) * 2 + core)
        gc_copy(k).wait_recv()

    def to_chip(k):
        chip_terms(k)
        xsend[k] = (keep[...] + crecv[k]).astype(BF16)
        gx_copy(k).start()

    loop(1, n_chips, to_chip)
    chip_terms(0)
    keep[...] += crecv[0]

    def add_x(k):
        gx_copy(k).wait_recv()
        keep[...] += xrecv[k].astype(F32)

    loop(1, n_chips, add_x)
    zsend[...] = keep[...].reshape(n_women, width, 128).astype(BF16)
    loop(1, n_women, lambda j: gz_copy(j).start())
    women_out[...] = keep[pl.ds(pl.multiple_of(w * width, width), width), :]

    def add_grad(j):
        gz_copy(j).wait_recv()
        women_out[...] += zrecv[j].astype(F32)

    loop(1, n_women, add_grad)

    def z_sends(j):
        z_copy(j).wait_send()
        root_copy(j).wait_send()
        cz_copy(j).wait_send()
        cg_copy(j).wait_send()
        gz_copy(j).wait_send()

    loop(1, n_women, z_sends)
    loop(1, n_men, lambda j: cp_copy(j).wait_send())
    loop(0, n_women, lambda j: loop(1, n_chips, lambda k: x_copy(k, j).wait_send()))
    loop(0, n_women, lambda j: loop(0, n_chips, lambda k: c_copy(k, j).wait_send()))
    loop(0, n_chips, lambda k: gc_copy(k).wait_send())
    loop(1, n_chips, lambda k: gx_copy(k).wait_send())


def body(
    n_men, n_women,
    men_embed, women_embed, men_count, women_count, women_root, men_cotangent, women_cotangent
):
    rows, emb = men_embed.shape
    width = women_embed.shape[0]
    group = n_women * width
    n_chips = n_men // 2
    dma = pltpu.SemaphoreType.DMA
    vmem = pl.BlockSpec(memory_space=pltpu.VMEM)
    quarter = (n_men, width)
    return pl.pallas_call(
        functools.partial(kernel, n_men, n_women),
        out_shape=(
            jax.ShapeDtypeStruct((rows, emb), F32),
            jax.ShapeDtypeStruct((width, emb), F32),
        ),
        in_specs=[vmem] * 7,
        out_specs=(vmem, vmem),
        scratch_shapes=[
            pltpu.VMEM((n_men, n_women, width, emb), BF16),
            pltpu.VMEM((n_men, rows, group), F32),
            pltpu.VMEM((n_women,) + quarter, F32),
            pltpu.VMEM((n_women,) + quarter, F32),
            pltpu.VMEM((n_men, group), F32),
            pltpu.VMEM((n_men, group), F32),
            pltpu.VMEM((n_men, group), F32),
            pltpu.VMEM((n_women,) + quarter, F32),
            pltpu.VMEM((n_women,) + quarter, F32),
            pltpu.VMEM((n_men,) + quarter, F32),
            pltpu.VMEM(quarter, F32),
            pltpu.VMEM((rows, emb), F32),
            pltpu.VMEM((rows, emb), F32),
            pltpu.VMEM((rows, 128), F32),
            pltpu.VMEM((rows, group), BF16),
            pltpu.VMEM((n_chips, group, emb), F32),
            pltpu.VMEM((n_chips, group, emb), F32),
            pltpu.VMEM((group, emb), F32),
            pltpu.VMEM((n_chips, group, emb), BF16),
            pltpu.VMEM((n_chips, group, emb), BF16),
            pltpu.VMEM((n_women, width, emb), BF16),
            pltpu.VMEM((n_women, width, emb), BF16),
            dma((n_men, n_women)),
            dma((n_women,)),
            dma((n_chips, n_women)),
            dma((n_chips, n_women)),
            dma((n_women,)), dma((n_women,)),
            dma((n_women,)), dma((n_women,)),
            dma((n_men,)), dma((n_men,)),
            dma((n_women,)), dma((n_women,)),
            dma((n_chips,)), dma((n_chips,)),
            dma((n_chips,)), dma((n_chips,)),
            dma((n_women,)), dma((n_women,)),
        ],
        compiler_params=pltpu.CompilerParams(
            collective_id=0, has_side_effects=True, vmem_limit_bytes=48 * 1024 * 1024,
        ),
        name="matching_backward",
    )(
        men_embed, women_embed,
        men_count.reshape(n_women, 1, rows), men_cotangent.reshape(n_women, 1, rows),
        women_root.reshape(quarter), women_count.reshape(quarter),
        women_cotangent.reshape(quarter),
    )


def solution(mesh):
    return jax.shard_map(
        functools.partial(body, mesh.shape["men"], mesh.shape["women"]),
        mesh=mesh,
        in_specs=(
            P(("men", "women"), None),
            P(("women", "men"), None),
            P("men"),
            P("women"),
            P("women"),
            P("men"),
            P("women"),
        ),
        out_specs=(P(("men", "women"), None), P(("women", "men"), None)),
        check_vma=False,
    )
```

time: 157 us -> 55.6 us (0.35)
  blocking collectives: 60.1 us -> 0 us
  waiting for transfers between devices: 51.8 us -> 0 us
  Pallas kernels: 0 us -> 48.1 us
  matrix products: 21.9 us -> 0 us
  between operations: 14.1 us -> 0.66 us
  other arithmetic: 8.05 us -> 0 us
  local copies, waits for them, and re-layouts: 0.02 us -> 6.44 us
    reduce_scatter x2 -> x0, waiting for transfers between devices: 51.8 us -> none  [the longest x1 30.1 us: body(): lax.psum_scatter(men_term, 'women', scatter_dimension=0, tiled=True)]
    pallas_call x0 -> x1, Pallas kernels: none -> 48.1 us  [body(): pl.pallas_call(functools.partial(kernel, n_men, n_women), out_shape=(jax....]
    psum x3 -> x0, blocking collectives: 32.5 us -> none  [the longest x1 12.2 us: body(): row_mass = lax.psum(row_partial, 'women')]
    all_gather x2 -> x0, blocking collectives: 27.5 us -> none  [the longest x1 16.6 us: body(): men_rows = lax.all_gather(men_embed, 'women', axis=0, tiled=True)]
    dot_general x4 -> x0, matrix products: 21.9 us -> none  [the longest x1 6.19 us: first_work(): jnp.dot(weighted.astype(jnp.bfloat16), women_block, preferred_element_typ...]
    reduce_sum x2 -> x0, other arithmetic: 8.01 us -> none  [the longest x1 4.01 us: second_work(): return ((), (jnp.sum(kernel * men_root[:, None], axis=0),))]
    unnamed x10 -> x16, local copies, waits for them, and re-layouts: 0.02 us -> 6.44 us
  transfers between devices with their start and end apart: 2 -> 0, of which waited for: 2 -> 0; matrix products, arithmetic and copies ran while one was open for 7% -> 0% of each run, Pallas kernels for 0% -> 0%
where the time goes in v1:
time: 55.6 us; the launch traced here: 55.2 us
  Pallas kernels  48.1 us (87%)
  local copies, waits for them, and re-layouts  6.44 us (12%)
  between operations  0.66 us (1%)
    pallas_call x1, Pallas kernels, body(): pl.pallas_call(functools.partial(kernel, n_men, n_women), out_shape=(jax....  48.1 us
    unnamed x16, local copies, waits for them, and re-layouts  6.44 us

profile of v1, /device:TPU:0, one launch (start us, length us, event | category | flops | bytes accessed | tf_op | source)
XLA Modules:
  0.0 55.2 jit_solution(5387981814177061960)
XLA Ops:
  0.6 0.0 copy-start.2
  0.6 0.7 %copy-done.2 = s32[2048]{0:T(1024)S(1)} copy-done((s32[2048]{0:T(1024)S(1)}, s32[2048]{0:T(1024)}, u32[]{:S(2)}) %copy-start.2) | copy-done | bytes 8216
  1.3 0.0 copy-start
  1.3 0.9 %copy-done = bf16[512,128]{1,0:T(8,128)(2,1)S(1)} copy-done((bf16[512,128]{1,0:T(8,128)(2,1)S(1)}, bf16[512,128]{1,0:T(8,128)(2,1)}, u32[]{:S(2)}) %copy-start) | copy-done | bytes 131096
  2.2 0.0 copy-start.1
  2.2 0.8 %copy-done.1 = bf16[128,128]{1,0:T(8,128)(2,1)S(1)} copy-done((bf16[128,128]{1,0:T(8,128)(2,1)S(1)}, bf16[128,128]{1,0:T(8,128)(2,1)}, u32[]{:S(2)}) %copy-start.1) | copy-done | bytes 32792
  3.0 0.0 copy-start.3
  3.0 0.7 %copy-done.3 = f32[2048]{0:T(1024)S(1)} copy-done((f32[2048]{0:T(1024)S(1)}, f32[2048]{0:T(1024)}, u32[]{:S(2)}) %copy-start.3) | copy-done | bytes 8216
  3.7 0.0 copy-start.4
  3.7 0.7 %copy-done.4 = f32[1024]{0:T(1024)S(1)} copy-done((f32[1024]{0:T(1024)S(1)}, f32[1024]{0:T(1024)}, u32[]{:S(2)}) %copy-start.4) | copy-done | bytes 4120
  4.4 0.0 copy-start.5
  4.4 0.7 %copy-done.5 = s32[1024]{0:T(1024)S(1)} copy-done((s32[1024]{0:T(1024)S(1)}, s32[1024]{0:T(1024)}, u32[]{:S(2)}) %copy-start.5) | copy-done | bytes 4120
  5.1 0.0 copy-start.6
  5.1 0.7 %copy-done.6 = f32[1024]{0:T(1024)S(1)} copy-done((f32[1024]{0:T(1024)S(1)}, f32[1024]{0:T(1024)}, u32[]{:S(2)}) %copy-start.6) | copy-done | bytes 4120
  5.8 48.1 %matching_backward.1 = (f32[512,128]{1,0:T(8,128)S(1)}, f32[128,128]{1,0:T(8,128)S(1)}) custom-call(bf16[512,128]{1,0:T(8,128)(2,1)S(1)} %copy-done, bf16[128,128]{1,0:T(8,128)(2,1)S(1)} %copy-done.1, s32[4,1,512]{2,1,0:T(1,128)S(1)} %bitcast.5, f32[4,1,512]{2,1,0:T(1,128)S(1)} %bitcast.6, f32[8,128]{1,0:T(8,128)S(1)} %bitcast.7, s32[8,128]{1,0:T(8,128)S(1)} %bitcast.8, ...), custom_call_target="tpu_custom_call" | custom-call | tf_op jit(solution)/shard_map/matching_backward/pallas_call | solution.py:309
  53.9 0.7 %copy.11 = f32[512,128]{1,0:T(8,128)} copy(f32[512,128]{1,0:T(8,128)S(1)} %get-tuple-element.4) | data formatting | bytes 524288
  54.6 0.6 %copy.12 = f32[128,128]{1,0:T(8,128)} copy(f32[128,128]{1,0:T(8,128)S(1)} %get-tuple-element.5) | data formatting | bytes 131072
Async XLA Ops:
  0.6 0.7 %copy-start.2 = (s32[2048]{0:T(1024)S(1)}, s32[2048]{0:T(1024)}, u32[]{:S(2)}) copy-start(s32[2048]{0:T(1024)} %param.9) | copy-start | bytes 24580
  1.3 0.9 %copy-start = (bf16[512,128]{1,0:T(8,128)(2,1)S(1)}, bf16[512,128]{1,0:T(8,128)(2,1)}, u32[]{:S(2)}) copy-start(bf16[512,128]{1,0:T(8,128)(2,1)} %men_ref.1) | copy-start | bytes 393220
  2.2 0.8 %copy-start.1 = (bf16[128,128]{1,0:T(8,128)(2,1)S(1)}, bf16[128,128]{1,0:T(8,128)(2,1)}, u32[]{:S(2)}) copy-start(bf16[128,128]{1,0:T(8,128)(2,1)} %women_ref.1) | copy-start | bytes 98308
  3.0 0.7 %copy-start.3 = (f32[2048]{0:T(1024)S(1)}, f32[2048]{0:T(1024)}, u32[]{:S(2)}) copy-start(f32[2048]{0:T(1024)} %param.12) | copy-start | bytes 24580
  3.7 0.7 %copy-start.4 = (f32[1024]{0:T(1024)S(1)}, f32[1024]{0:T(1024)}, u32[]{:S(2)}) copy-start(f32[1024]{0:T(1024)} %param.11) | copy-start | bytes 12292
  4.4 0.7 %copy-start.5 = (s32[1024]{0:T(1024)S(1)}, s32[1024]{0:T(1024)}, u32[]{:S(2)}) copy-start(s32[1024]{0:T(1024)} %param.10) | copy-start | bytes 12292
  5.1 0.7 %copy-start.6 = (f32[1024]{0:T(1024)S(1)}, f32[1024]{0:T(1024)}, u32[]{:S(2)}) copy-start(f32[1024]{0:T(1024)} %param.13) | copy-start | bytes 12292

commit v2 on v1

--- a/solution.py
+++ b/solution.py
@@ -24,16 +24,17 @@
 
 def kernel(
     n_men, n_women,
-    men_ref, women_ref, count_ref, cot_ref, root_ref, wcount_ref, wcot_ref,
+    men_hbm, women_hbm, count_hbm, cot_hbm, root_hbm, wcount_hbm, wcot_hbm,
     men_out, women_out,
-    wbuf, kmat, rootbuf, gradbuf, rootg, gradg, colp, pieces, zsum, psum_, quarter,
+    men_ref, count_ref, cot_ref, wbuf, kmat, rootbuf, wcountbuf, wcotbuf,
+    rootg, wcountg, wcotg, gradg, colp, colrecv, zpart,
     wv, dv, rsum, tang, csend, crecv, keep, xsend, xrecv, zsend, zrecv,
-    ag_recv, ag_zsend, ag_xsend, ag_csend,
+    local, ag_recv, ag_zsend, ag_xsend, ag_csend,
     root_send, root_recv, cz_send, cz_recv, cp_send, cp_recv, cg_send, cg_recv,
     gc_send, gc_recv, gx_send, gx_recv, gz_send, gz_recv,
 ):
-    rows = men_ref.shape[0]
-    width = women_ref.shape[0]
+    rows = men_hbm.shape[0]
+    width = women_hbm.shape[0]
     group = n_women * width
     n_chips = n_men // 2
     chunk = min(rows, 128)
@@ -61,13 +62,23 @@
             device_id=(to_m, to_w), device_id_type=MESH,
         )
 
+    fetches = [
+        pltpu.make_async_copy(src, dst, local.at[i])
+        for i, (src, dst) in enumerate((
+            (women_hbm, wbuf.at[m, w]), (root_hbm, rootbuf.at[w]),
+            (wcount_hbm, wcountbuf.at[w]), (wcot_hbm, wcotbuf.at[w]),
+            (men_hbm, men_ref), (count_hbm.at[w], count_ref), (cot_hbm.at[w], cot_ref),
+        ))
+    ]
+    for fetch in fetches:
+        fetch.start()
+
     barrier = pltpu.get_barrier_semaphore()
     loop(1, n_women, lambda j: pl.semaphore_signal(
         barrier, inc=1, device_id=(m, z_to(j)), device_id_type=MESH))
     loop(1, n_men, lambda j: pl.semaphore_signal(
         barrier, inc=1, device_id=(lax.rem(m + j, n_men), w), device_id_type=MESH))
-    wbuf[m, w] = women_ref[...]
-    rootbuf[w] = root_ref[...]
+    fetches[0].wait()
     pl.semaphore_wait(barrier, n_women + n_men - 2)
 
     def block_copy(at_m, at_w, send, to_m, to_w):
@@ -86,19 +97,26 @@
     def landed(at_m, at_w):
         block_copy(at_m, at_w, ag_zsend.at[0], sib, w).wait_recv()
 
-    def root_copy(j):
-        return copy(rootbuf.at[w], rootbuf.at[w], root_send.at[j], root_recv.at[j], m, z_to(j))
+    def vector_copies(j):
+        return [copy(buf.at[w], buf.at[w], root_send.at[i, j], root_recv.at[i, j], m, z_to(j))
+                for i, buf in enumerate((rootbuf, wcountbuf, wcotbuf))]
+
+    def each(copies, act):
+        for one in copies:
+            getattr(one, act)()
 
     loop(1, n_women, lambda j: z_copy(j).start())
     loop(1, n_chips, lambda k: x_copy(k, 0).start())
-    loop(1, n_women, lambda j: root_copy(j).start())
     c_copy(0, 0).start()
+    for fetch in fetches[1:]:
+        fetch.wait()
+    loop(1, n_women, lambda j: each(vector_copies(j), "start"))
 
     def column(row):
         return jnp.broadcast_to(row, (128, rows)).T
 
-    mass = column(count_ref[w].astype(F32))
-    men_cot = column(cot_ref[w])
+    mass = column(count_ref[...].astype(F32))
+    men_cot = column(cot_ref[...])
     men_t = men_ref[...].astype(F32).T.astype(BF16)
     rsum[...] = jnp.zeros_like(rsum)
     wv[...] = jnp.zeros_like(wv)
@@ -109,13 +127,15 @@
         c_copy(0, j).start()
 
     loop(1, n_women, pass_on)
-    loop(1, n_women, lambda j: root_copy(j).wait_recv())
+    loop(1, n_women, lambda j: each(vector_copies(j), "wait_recv"))
 
     def spread(buf, out):
         for i in range(n_women):
             out[:, i * width:(i + 1) * width] = buf[i]
 
     spread(rootbuf, rootg)
+    spread(wcountbuf, wcountg)
+    spread(wcotbuf, wcotg)
 
     def lanes(values):
         total = values[:, :128]
@@ -171,60 +191,64 @@
         for r in range(0, rows, chunk):
             term = kmat[g, pl.ds(r, chunk), :] * wide(men_root[r:r + chunk])
             total = total + jnp.sum(term.reshape(chunk // 8, 8, group), axis=0)
-        colp[pl.ds(g, 1), :] = jnp.sum(total, axis=0, keepdims=True)
-
-    loop(0, n_men, second)
-
-    for i in range(n_women):
-        pieces[i] = colp[:, i * width:(i + 1) * width]
+        colp[g] = jnp.sum(total, axis=0, keepdims=True)
+
+    def near(j):
+        return lax.rem(m + j, n_men)
+
+    def cp_copy(j):
+        return copy(colp.at[near(j)], colrecv.at[j], cp_send.at[j], cp_recv.at[j], near(j), w)
 
     def cz_copy(j):
-        return copy(pieces.at[z_to(j)], zsum.at[j], cz_send.at[j], cz_recv.at[j], m, z_to(j))
-
+        return copy(zpart.at[0], zpart.at[j], cz_send.at[j], cz_recv.at[j], m, z_to(j))
+
+    def cg_copy(j):
+        return copy(gradg.at[m], gradg.at[m], cg_send.at[j], cg_recv.at[j], near(j), w)
+
+    def for_owner(j):
+        second(near(j))
+        cp_copy(j).start()
+
+    loop(1, n_men, for_owner)
+    second(m)
+    zpart[0] = colp[m]
+    rsum[...] = jnp.zeros_like(rsum)
+    dv[...] = jnp.zeros_like(dv)
+
+    def add_p(j):
+        cp_copy(j).wait_recv()
+        zpart[0] += colrecv[j]
+
+    loop(1, n_men, add_p)
     loop(1, n_women, lambda j: cz_copy(j).start())
-    quarter[...] = pieces[w]
+    colp[m] = zpart[0]
 
     def add_z(j):
         cz_copy(j).wait_recv()
-        quarter[...] += zsum[j]
+        colp[m] += zpart[j]
 
     loop(1, n_women, add_z)
-
-    def cp_copy(j):
-        return copy(quarter, psum_.at[j], cp_send.at[j], cp_recv.at[j],
-                    lax.rem(m + j, n_men), w)
-
-    loop(1, n_men, lambda j: cp_copy(j).start())
-    psum_[0] = quarter[...]
-
-    def add_p(j):
-        cp_copy(j).wait_recv()
-        psum_[0] += psum_[j]
-
-    loop(1, n_men, add_p)
-    col_mass = psum_[0]
-    women_disc = jnp.sqrt(col_mass * col_mass + 4.0 * wcount_ref[...].astype(F32))
-    gradbuf[w] = -wcot_ref[...] / women_disc
-
-    def cg_copy(j):
-        return copy(gradbuf.at[w], gradbuf.at[w], cg_send.at[j], cg_recv.at[j], m, z_to(j))
-
-    loop(1, n_women, lambda j: cg_copy(j).start())
-    rsum[...] = jnp.zeros_like(rsum)
-    dv[...] = jnp.zeros_like(dv)
-    loop(1, n_women, lambda j: cg_copy(j).wait_recv())
-    spread(gradbuf, gradg)
+    col_mass = colp[m]
+    women_mass = wcountg[pl.ds(m, 1), :].astype(F32)
+    women_disc = jnp.sqrt(col_mass * col_mass + 4.0 * women_mass)
+    gradg[m] = -wcotg[pl.ds(m, 1), :] / women_disc
+    loop(1, n_men, lambda j: cg_copy(j).start())
 
     def third(g):
         block = wbuf[g].reshape(group, 128)
-        grads = gradg[pl.ds(g, 1), :]
+        grads = gradg[g]
         for r in range(0, rows, chunk):
             at = pl.ds(r, chunk)
             weighted = kmat[g, at, :] * grads
             rsum[at, :] += lanes(weighted)
             dv[at, :] += jnp.dot(weighted.astype(BF16), block, preferred_element_type=F32)
 
-    loop(0, n_men, third)
+    def third_from(j):
+        cg_copy(j).wait_recv()
+        third(lax.rem(m + n_men - j, n_men))
+
+    third(m)
+    loop(1, n_men, third_from)
     row_cot = jnp.broadcast_to(jnp.sum(rsum[...], axis=1, keepdims=True), (rows, 128))
     row_grad = -(men_cot + men_root * row_cot) / men_disc
     half_grad = 0.5 * row_grad
@@ -233,7 +257,7 @@
 
     def fourth(g):
         roots = rootg[pl.ds(g, 1), :]
-        grads = gradg[pl.ds(g, 1), :]
+        grads = gradg[g]
         for r in range(0, rows, chunk):
             at = pl.ds(r, chunk)
             scale = wide(half_grad[r:r + chunk]) * roots + wide(half_root[r:r + chunk]) * grads
@@ -243,12 +267,12 @@
     def gc_copy(k):
         return copy(csend.at[k], crecv.at[k], gc_send.at[k], gc_recv.at[k], sib, w)
 
-    def gx_copy(k):
-        return copy(xsend.at[k], xrecv.at[k], gx_send.at[k], gx_recv.at[k],
-                    chip_to(k) * 2 + core, w)
+    def gx_copy(k, j):
+        return copy(xsend.at[k, z_to(j)], xrecv.at[k, z_to(j)], gx_send.at[k, j],
+                    gx_recv.at[k, j], chip_to(k) * 2 + core, w)
 
     def gz_copy(j):
-        return copy(zsend.at[z_to(j)], zrecv.at[j], gz_send.at[j], gz_recv.at[j], m, z_to(j))
+        return copy(zsend.at[j], zrecv.at[j], gz_send.at[j], gz_recv.at[j], m, z_to(j))
 
     def chip_terms(k):
         csend[k] = fourth(chip_to(k) * 2 + (1 - core))
@@ -258,21 +282,30 @@
 
     def to_chip(k):
         chip_terms(k)
-        xsend[k] = (keep[...] + crecv[k]).astype(BF16)
-        gx_copy(k).start()
+        xsend[k] = (keep[...] + crecv[k]).reshape(n_women, width, 128).astype(BF16)
+        loop(1, n_women, lambda j: gx_copy(k, j).start())
+        gx_copy(k, 0).start()
 
     loop(1, n_chips, to_chip)
     chip_terms(0)
     keep[...] += crecv[0]
 
-    def add_x(k):
-        gx_copy(k).wait_recv()
-        keep[...] += xrecv[k].astype(F32)
-
-    loop(1, n_chips, add_x)
-    zsend[...] = keep[...].reshape(n_women, width, 128).astype(BF16)
-    loop(1, n_women, lambda j: gz_copy(j).start())
-    women_out[...] = keep[pl.ds(pl.multiple_of(w * width, width), width), :]
+    def part(j):
+        return keep.at[pl.ds(pl.multiple_of(z_to(j) * width, width), width), :]
+
+    def add_x(j):
+        loop(1, n_chips, lambda k: gx_copy(k, j).wait_recv())
+        total = part(j)[...]
+        for k in range(1, n_chips):
+            total = total + xrecv[k, z_to(j)].astype(F32)
+        return total
+
+    def along_z(j):
+        zsend[j] = add_x(j).astype(BF16)
+        gz_copy(j).start()
+
+    loop(1, n_women, along_z)
+    women_out[...] = add_x(0)
 
     def add_grad(j):
         gz_copy(j).wait_recv()
@@ -282,17 +315,17 @@
 
     def z_sends(j):
         z_copy(j).wait_send()
-        root_copy(j).wait_send()
+        each(vector_copies(j), "wait_send")
         cz_copy(j).wait_send()
-        cg_copy(j).wait_send()
         gz_copy(j).wait_send()
 
     loop(1, n_women, z_sends)
     loop(1, n_men, lambda j: cp_copy(j).wait_send())
+    loop(1, n_men, lambda j: cg_copy(j).wait_send())
     loop(0, n_women, lambda j: loop(1, n_chips, lambda k: x_copy(k, j).wait_send()))
     loop(0, n_women, lambda j: loop(0, n_chips, lambda k: c_copy(k, j).wait_send()))
     loop(0, n_chips, lambda k: gc_copy(k).wait_send())
-    loop(1, n_chips, lambda k: gx_copy(k).wait_send())
+    loop(0, n_women, lambda j: loop(1, n_chips, lambda k: gx_copy(k, j).wait_send()))
 
 
 def body(
@@ -312,20 +345,24 @@
             jax.ShapeDtypeStruct((rows, emb), F32),
             jax.ShapeDtypeStruct((width, emb), F32),
         ),
-        in_specs=[vmem] * 7,
+        in_specs=[pl.BlockSpec(memory_space=pltpu.HBM)] * 7,
         out_specs=(vmem, vmem),
         scratch_shapes=[
+            pltpu.VMEM((rows, emb), BF16),
+            pltpu.VMEM((1, rows), jnp.int32),
+            pltpu.VMEM((1, rows), F32),
             pltpu.VMEM((n_men, n_women, width, emb), BF16),
             pltpu.VMEM((n_men, rows, group), F32),
             pltpu.VMEM((n_women,) + quarter, F32),
+            pltpu.VMEM((n_women,) + quarter, jnp.int32),
             pltpu.VMEM((n_women,) + quarter, F32),
             pltpu.VMEM((n_men, group), F32),
+            pltpu.VMEM((n_men, group), jnp.int32),
             pltpu.VMEM((n_men, group), F32),
-            pltpu.VMEM((n_men, group), F32),
-            pltpu.VMEM((n_women,) + quarter, F32),
-            pltpu.VMEM((n_women,) + quarter, F32),
-            pltpu.VMEM((n_men,) + quarter, F32),
-            pltpu.VMEM(quarter, F32),
+            pltpu.VMEM((n_men, 1, group), F32),
+            pltpu.VMEM((n_men, 1, group), F32),
+            pltpu.VMEM((n_men, 1, group), F32),
+            pltpu.VMEM((n_women, 1, group), F32),
             pltpu.VMEM((rows, emb), F32),
             pltpu.VMEM((rows, emb), F32),
             pltpu.VMEM((rows, 128), F32),
@@ -333,20 +370,21 @@
             pltpu.VMEM((n_chips, group, emb), F32),
             pltpu.VMEM((n_chips, group, emb), F32),
             pltpu.VMEM((group, emb), F32),
-            pltpu.VMEM((n_chips, group, emb), BF16),
-            pltpu.VMEM((n_chips, group, emb), BF16),
+            pltpu.VMEM((n_chips, n_women, width, emb), BF16),
+            pltpu.VMEM((n_chips, n_women, width, emb), BF16),
             pltpu.VMEM((n_women, width, emb), BF16),
             pltpu.VMEM((n_women, width, emb), BF16),
+            dma((7,)),
             dma((n_men, n_women)),
             dma((n_women,)),
             dma((n_chips, n_women)),
             dma((n_chips, n_women)),
-            dma((n_women,)), dma((n_women,)),
+            dma((3, n_women)), dma((3, n_women)),
             dma((n_women,)), dma((n_women,)),
             dma((n_men,)), dma((n_men,)),
-            dma((n_women,)), dma((n_women,)),
+            dma((n_men,)), dma((n_men,)),
             dma((n_chips,)), dma((n_chips,)),
-            dma((n_chips,)), dma((n_chips,)),
+            dma((n_chips, n_women)), dma((n_chips, n_women)),
             dma((n_women,)), dma((n_women,)),
         ],
         compiler_params=pltpu.CompilerParams(

time: 55.6 us -> 53.8 us (0.968)
  Pallas kernels: 48.1 us -> 46.4 us
    pallas_call x1, Pallas kernels: 48.1 us -> 46.4 us  [body(): pl.pallas_call(functools.partial(kernel, n_men, n_women), out_shape=(jax....]
where the time goes in v2:
time: 53.8 us; the launch traced here: 53.5 us
  Pallas kernels  46.4 us (86%)
  local copies, waits for them, and re-layouts  6.44 us (12%)
  between operations  0.66 us (1%)
    pallas_call x1, Pallas kernels, body(): pl.pallas_call(functools.partial(kernel, n_men, n_women), out_shape=(jax....  46.4 us
    unnamed x16, local copies, waits for them, and re-layouts  6.44 us

profile of v2, /device:TPU:0, one launch (start us, length us, event | category | flops | bytes accessed | tf_op | source)
XLA Modules:
  0.0 53.5 jit_solution(8273566288263473804)
XLA Ops:
  0.6 0.0 copy-start.2
  0.6 0.7 %copy-done.2 = s32[2048]{0:T(1024)S(1)} copy-done((s32[2048]{0:T(1024)S(1)}, s32[2048]{0:T(1024)}, u32[]{:S(2)}) %copy-start.2) | copy-done | bytes 8216
  1.3 0.0 copy-start
  1.3 0.9 %copy-done = bf16[512,128]{1,0:T(8,128)(2,1)S(1)} copy-done((bf16[512,128]{1,0:T(8,128)(2,1)S(1)}, bf16[512,128]{1,0:T(8,128)(2,1)}, u32[]{:S(2)}) %copy-start) | copy-done | bytes 131096
  2.2 0.0 copy-start.1
  2.2 0.8 %copy-done.1 = bf16[128,128]{1,0:T(8,128)(2,1)S(1)} copy-done((bf16[128,128]{1,0:T(8,128)(2,1)S(1)}, bf16[128,128]{1,0:T(8,128)(2,1)}, u32[]{:S(2)}) %copy-start.1) | copy-done | bytes 32792
  3.0 0.0 copy-start.3
  3.0 0.7 %copy-done.3 = f32[2048]{0:T(1024)S(1)} copy-done((f32[2048]{0:T(1024)S(1)}, f32[2048]{0:T(1024)}, u32[]{:S(2)}) %copy-start.3) | copy-done | bytes 8216
  3.7 0.0 copy-start.4
  3.7 0.7 %copy-done.4 = f32[1024]{0:T(1024)S(1)} copy-done((f32[1024]{0:T(1024)S(1)}, f32[1024]{0:T(1024)}, u32[]{:S(2)}) %copy-start.4) | copy-done | bytes 4120
  4.4 0.0 copy-start.5
  4.4 0.7 %copy-done.5 = s32[1024]{0:T(1024)S(1)} copy-done((s32[1024]{0:T(1024)S(1)}, s32[1024]{0:T(1024)}, u32[]{:S(2)}) %copy-start.5) | copy-done | bytes 4120
  5.1 0.0 copy-start.6
  5.1 0.7 %copy-done.6 = f32[1024]{0:T(1024)S(1)} copy-done((f32[1024]{0:T(1024)S(1)}, f32[1024]{0:T(1024)}, u32[]{:S(2)}) %copy-start.6) | copy-done | bytes 4120
  5.8 46.4 %matching_backward.1 = (f32[512,128]{1,0:T(8,128)S(1)}, f32[128,128]{1,0:T(8,128)S(1)}) custom-call(bf16[512,128]{1,0:T(8,128)(2,1)S(1)} %copy-done, bf16[128,128]{1,0:T(8,128)(2,1)S(1)} %copy-done.1, s32[4,1,512]{2,1,0:T(1,128)S(1)} %bitcast.5, f32[4,1,512]{2,1,0:T(1,128)S(1)} %bitcast.6, f32[8,128]{1,0:T(8,128)S(1)} %bitcast.7, s32[8,128]{1,0:T(8,128)S(1)} %bitcast.8, ...), custom_call_target="tpu_custom_call" | custom-call | tf_op jit(solution)/shard_map/matching_backward/pallas_call | solution.py:342
  52.1 0.7 %copy.11 = f32[512,128]{1,0:T(8,128)} copy(f32[512,128]{1,0:T(8,128)S(1)} %get-tuple-element.4) | data formatting | bytes 524288
  52.8 0.6 %copy.12 = f32[128,128]{1,0:T(8,128)} copy(f32[128,128]{1,0:T(8,128)S(1)} %get-tuple-element.5) | data formatting | bytes 131072
Async XLA Ops:
  0.6 0.7 %copy-start.2 = (s32[2048]{0:T(1024)S(1)}, s32[2048]{0:T(1024)}, u32[]{:S(2)}) copy-start(s32[2048]{0:T(1024)} %param.9) | copy-start | bytes 24580
  1.3 0.9 %copy-start = (bf16[512,128]{1,0:T(8,128)(2,1)S(1)}, bf16[512,128]{1,0:T(8,128)(2,1)}, u32[]{:S(2)}) copy-start(bf16[512,128]{1,0:T(8,128)(2,1)} %men_hbm.1) | copy-start | bytes 393220
  2.2 0.8 %copy-start.1 = (bf16[128,128]{1,0:T(8,128)(2,1)S(1)}, bf16[128,128]{1,0:T(8,128)(2,1)}, u32[]{:S(2)}) copy-start(bf16[128,128]{1,0:T(8,128)(2,1)} %women_hbm.1) | copy-start | bytes 98308
  3.0 0.7 %copy-start.3 = (f32[2048]{0:T(1024)S(1)}, f32[2048]{0:T(1024)}, u32[]{:S(2)}) copy-start(f32[2048]{0:T(1024)} %param.12) | copy-start | bytes 24580
  3.7 0.7 %copy-start.4 = (f32[1024]{0:T(1024)S(1)}, f32[1024]{0:T(1024)}, u32[]{:S(2)}) copy-start(f32[1024]{0:T(1024)} %param.11) | copy-start | bytes 12292
  4.4 0.7 %copy-start.5 = (s32[1024]{0:T(1024)S(1)}, s32[1024]{0:T(1024)}, u32[]{:S(2)}) copy-start(s32[1024]{0:T(1024)} %param.10) | copy-start | bytes 12292
  5.1 0.7 %copy-start.6 = (f32[1024]{0:T(1024)S(1)}, f32[1024]{0:T(1024)}, u32[]{:S(2)}) copy-start(f32[1024]{0:T(1024)} %param.13) | copy-start | bytes 12292

commit v3 on v2

--- a/solution.py
+++ b/solution.py
@@ -37,7 +37,7 @@
     width = women_hbm.shape[0]
     group = n_women * width
     n_chips = n_men // 2
-    chunk = min(rows, 128)
+    chunk = min(rows, 256)
     m = lax.axis_index("men")
     w = lax.axis_index("women")
     c = m // 2
@@ -51,9 +51,13 @@
         return lax.rem(w + n_women - j, n_women)
 
     def chip_to(k):
+        if n_chips == 4:
+            return (c // 2 + k // 2) % 2 * 2 + (c + k) % 2
         return lax.rem(c + k, n_chips)
 
     def chip_from(k):
+        if n_chips == 4:
+            return chip_to(k)
         return lax.rem(c + n_chips - k, n_chips)
 
     def copy(src, dst, send, recv, to_m, to_w):
@@ -106,7 +110,7 @@
             getattr(one, act)()
 
     loop(1, n_women, lambda j: z_copy(j).start())
-    loop(1, n_chips, lambda k: x_copy(k, 0).start())
+    loop(1, n_chips, lambda k: x_copy(n_chips - k, 0).start())
     c_copy(0, 0).start()
     for fetch in fetches[1:]:
         fetch.wait()
@@ -123,7 +127,7 @@
 
     def pass_on(j):
         landed(m, z_from(j))
-        loop(1, n_chips, lambda k: x_copy(k, j).start())
+        loop(1, n_chips, lambda k: x_copy(n_chips - k, j).start())
         c_copy(0, j).start()
 
     loop(1, n_women, pass_on)
@@ -286,7 +290,7 @@
         loop(1, n_women, lambda j: gx_copy(k, j).start())
         gx_copy(k, 0).start()
 
-    loop(1, n_chips, to_chip)
+    loop(1, n_chips, lambda k: to_chip(n_chips - k))
     chip_terms(0)
     keep[...] += crecv[0]
 
@@ -388,7 +392,7 @@
             dma((n_women,)), dma((n_women,)),
         ],
         compiler_params=pltpu.CompilerParams(
-            collective_id=0, has_side_effects=True, vmem_limit_bytes=48 * 1024 * 1024,
+            collective_id=0, has_side_effects=True, vmem_limit_bytes=60 * 1024 * 1024,
         ),
         name="matching_backward",
     )(

time: 53.8 us -> 48.8 us (0.907)
  local copies, waits for them, and re-layouts: 6.44 us -> 2.33 us
  Pallas kernels: 46.4 us -> 45.7 us
    unnamed x16 -> x4, local copies, waits for them, and re-layouts: 6.44 us -> 2.33 us
    pallas_call x1, Pallas kernels: 46.4 us -> 45.7 us  [body(): pl.pallas_call(functools.partial(kernel, n_men, n_women), out_shape=(jax....]
where the time goes in v3:
time: 48.8 us; the launch traced here: 48.7 us
  Pallas kernels  45.7 us (94%)
  local copies, waits for them, and re-layouts  2.33 us (5%)
  between operations  0.65 us (1%)
    pallas_call x1, Pallas kernels, body(): pl.pallas_call(functools.partial(kernel, n_men, n_women), out_shape=(jax....  45.7 us
    unnamed x4, local copies, waits for them, and re-layouts  2.33 us

profile of v3, /device:TPU:0, one launch (start us, length us, event | category | flops | bytes accessed | tf_op | source)
XLA Modules:
  0.0 48.7 jit_solution(8945160525196970225)
XLA Ops:
  0.6 45.7 %matching_backward.1 = (f32[512,128]{1,0:T(8,128)}, f32[128,128]{1,0:T(8,128)}) custom-call(bf16[512,128]{1,0:T(8,128)(2,1)} %men_hbm.1, bf16[128,128]{1,0:T(8,128)(2,1)} %women_hbm.1, s32[4,1,512]{2,1,0:T(1,128)} %bitcast.5, f32[4,1,512]{2,1,0:T(1,128)} %bitcast.6, f32[8,128]{1,0:T(8,128)} %bitcast.7, s32[8,128]{1,0:T(8,128)} %bitcast.8, f32[8,128]{1,0:T(8,128)} %bitcast.9), custom_call_target="tpu_custom_call" | custom-call | tf_op jit(solution)/shard_map/matching_backward/pallas_call | solution.py:346
  46.3 0.0 copy-start
  46.3 1.7 %copy.11 = f32[512,128]{1,0:T(8,128)} copy(f32[512,128]{1,0:T(8,128)} %get-tuple-element.4) | data formatting | bytes 524288
  48.0 0.0 copy-done
  48.0 0.6 %copy.12 = f32[128,128]{1,0:T(8,128)} copy(f32[128,128]{1,0:T(8,128)S(1)} %copy-done) | data formatting | bytes 131072
Async XLA Ops:
  46.3 1.7 %copy-start = (f32[128,128]{1,0:T(8,128)S(1)}, f32[128,128]{1,0:T(8,128)}, u32[]{:S(2)}) copy-start(f32[128,128]{1,0:T(8,128)} %get-tuple-element.5) | copy-start | bytes 196612

commit v4 on v3

--- a/solution.py
+++ b/solution.py
@@ -37,7 +37,7 @@
     width = women_hbm.shape[0]
     group = n_women * width
     n_chips = n_men // 2
-    chunk = min(rows, 256)
+    chunk = min(rows, 512)
     m = lax.axis_index("men")
     w = lax.axis_index("women")
     c = m // 2

time: 48.8 us -> 47.8 us (0.980)
  Pallas kernels: 45.7 us -> 44.6 us
    pallas_call x1, Pallas kernels: 45.7 us -> 44.6 us  [body(): pl.pallas_call(functools.partial(kernel, n_men, n_women), out_shape=(jax....]
where the time goes in v4:
time: 47.8 us; the launch traced here: 47.6 us
  Pallas kernels  44.6 us (93%)
  local copies, waits for them, and re-layouts  2.33 us (5%)
  between operations  0.65 us (1%)
    pallas_call x1, Pallas kernels, body(): pl.pallas_call(functools.partial(kernel, n_men, n_women), out_shape=(jax....  44.6 us
    unnamed x4, local copies, waits for them, and re-layouts  2.33 us

profile of v4, /device:TPU:0, one launch (start us, length us, event | category | flops | bytes accessed | tf_op | source)
XLA Modules:
  0.0 47.6 jit_solution(3561899071395634056)
XLA Ops:
  0.6 44.6 %matching_backward.1 = (f32[512,128]{1,0:T(8,128)}, f32[128,128]{1,0:T(8,128)}) custom-call(bf16[512,128]{1,0:T(8,128)(2,1)} %men_hbm.1, bf16[128,128]{1,0:T(8,128)(2,1)} %women_hbm.1, s32[4,1,512]{2,1,0:T(1,128)} %bitcast.5, f32[4,1,512]{2,1,0:T(1,128)} %bitcast.6, f32[8,128]{1,0:T(8,128)} %bitcast.7, s32[8,128]{1,0:T(8,128)} %bitcast.8, f32[8,128]{1,0:T(8,128)} %bitcast.9), custom_call_target="tpu_custom_call" | custom-call | tf_op jit(solution)/shard_map/matching_backward/pallas_call | solution.py:346
  45.3 0.0 copy-start
  45.3 1.7 %copy.11 = f32[512,128]{1,0:T(8,128)} copy(f32[512,128]{1,0:T(8,128)} %get-tuple-element.4) | data formatting | bytes 524288
  47.0 0.0 copy-done
  47.0 0.6 %copy.12 = f32[128,128]{1,0:T(8,128)} copy(f32[128,128]{1,0:T(8,128)S(1)} %copy-done) | data formatting | bytes 131072
Async XLA Ops:
  45.3 1.7 %copy-start = (f32[128,128]{1,0:T(8,128)S(1)}, f32[128,128]{1,0:T(8,128)}, u32[]{:S(2)}) copy-start(f32[128,128]{1,0:T(8,128)} %get-tuple-element.5) | copy-start | bytes 196612
